TPU v7x, 32 devices: a whole 2x2x4 slice. The times are simulated.
32 devices in a mesh: col: 4 (over z), row: 8 (over y, x, core).
Axes of the slice: x: 2, y: 2, z: 4, core: 2. Of those that a mesh axis runs over, the one named last changes fastest.
Arguments:
- factor: float32 [8192, 2048], P('row', 'col'), may hold values from -100 to 100
- support: int32 [16, 64], P(None, 'row'), may hold values from 0 to 1, as said below
- plan: int32 [2, 16], replicated, may hold values from 0 to 15, as said below
Outputs:
- rotated_factor: float32 [8192, 2048], P('row', 'col')
Inputs may be any that keep to these rules, and one draw needn't show every extreme that they name: Every column block has at least one row block in its support. `plan`: each row is a permutation; cut each round's row into groups of 4 consecutive positions (group g on index g of col); the 4 blocks of any group sit in 4 different groups of the previous round's row, where the order before round 0 is 0, 1, ..., 15.
All inputs are finite; a program needn't handle non-finite values.
Results may differ from a plain program's by a relative error of at most 0.0003.
Values sent between devices are 32-bit elements; how exact they have to be, the bound alone decides.
A program may use at most 128 MiB of HBM per device.

v0:
```python
import jax
import jax.numpy as jnp
from jax import lax
from jax.sharding import PartitionSpec as P

W = 128
RB = 128
ROUNDS = 2


precise = lax.Precision.HIGHEST
damping = 0.01


def skew_terms(gram_rows, diag_rows, diag_cols):
    spread = diag_rows[:, :, None] - diag_cols[:, None, :]
    joined = diag_rows[:, :, None] + diag_cols[:, None, :]
    return (
        gram_rows * spread / (spread * spread + gram_rows * gram_rows + damping * joined * joined)
    )


def cayley(skew_matrix):
    size_here = skew_matrix.shape[0]
    identity = jnp.eye(size_here, dtype=jnp.float32)
    halved = 0.5 * skew_matrix
    minus_half = identity - halved
    numerator = jnp.dot(minus_half, minus_half, precision=precise)
    definite = identity + jnp.dot(halved.T, halved, precision=precise)
    lower_factor = jnp.linalg.cholesky(definite)
    return jax.scipy.linalg.cho_solve((lower_factor, True), numerator)


def local_gram(left_cols, right_cols):
    return jnp.einsum("rpi,rpj->pij", left_cols, right_cols, precision=precise)


def on_device(factor, support, plan):
    rows_here = factor.shape[0]
    slot_count = factor.shape[1] // W
    group_count = lax.axis_size("col")
    col_place = lax.axis_index("col")
    pair_count = slot_count // 2
    own_support = lax.dynamic_slice_in_dim(support, col_place * slot_count, slot_count, 0)
    row_mask = jnp.repeat(own_support.T, RB, axis=0).astype(jnp.float32)
    current = factor.reshape(rows_here, slot_count, W) * row_mask[:, :, None]
    previous = jnp.arange(slot_count * group_count, dtype=jnp.int32)
    my_slots = col_place * slot_count + jnp.arange(slot_count, dtype=jnp.int32)
    group_ids = jnp.arange(group_count, dtype=jnp.int32)
    for round_index in range(ROUNDS):
        order_now = plan[round_index]
        located = jnp.argsort(previous)[order_now]
        wanted = located[my_slots]
        new_place = jnp.argsort(order_now)[previous[my_slots]]
        send_pick = (new_place[None, :] // slot_count == group_ids[:, None]).astype(jnp.float32)
        outgoing = jnp.einsum("dt,rtw->rdw", send_pick, current, precision=precise)
        incoming = lax.all_to_all(outgoing, "col", split_axis=1, concat_axis=1, tiled=True)
        take_pick = (wanted[:, None] // slot_count == group_ids[None, :]).astype(jnp.float32)
        arranged = jnp.einsum("sd,rdw->rsw", take_pick, incoming, precision=precise)
        paired = arranged.reshape(rows_here, pair_count, 2 * W)
        gram_matrix = lax.psum(local_gram(paired, paired), "row")
        diagonal_terms = jnp.diagonal(gram_matrix, axis1=1, axis2=2)
        skew_matrix = skew_terms(gram_matrix, diagonal_terms, diagonal_terms)
        rotations = jax.vmap(cayley)(skew_matrix)
        rotated = jnp.einsum("rpi,pij->rpj", paired, rotations, precision=precise)
        current = rotated.reshape(rows_here, slot_count, W)
        previous = order_now
    return current.reshape(rows_here, slot_count * W)


def solution(mesh):
    return jax.shard_map(
        on_device,
        mesh=mesh,
        in_specs=(P("row", "col"), P(None, "row"), P()),
        out_specs=P("row", "col"),
        check_vma=False,
    )
```

profile of v0, /device:TPU:25, one launch (start us, length us, event | category | flops | bytes accessed | tf_op | source)
XLA Modules:
  0.0 562.9 jit_solution(1841204664896612224)
XLA Ops:
  8.6 1.2 sort.47
  9.9 1.9 reshape.293
  11.8 1.2 sort.49
  14.5 4.0 fusion.14
  18.5 1.5 copy.118
  20.0 4.7 all-to-all-start
  24.6 1.3 sort.48
  27.3 42.5 %all-to-all-done = f32[1024,4,128]{2,0,1:T(8,128)S(1)} async-done(((f32[1024,4,128]{2,0,1:T(8,128)}), f32[1024,4,128]{2,0,1:T(8,128)S(1)}, u32[]{:S(2)}, u32[]{:S(2)}) %all-to-all-start) | async-done | bytes 2097184 | tf_op jit(solution)/shard_map/all_to_all | solution.py:57
  69.8 4.6 fusion.17
  74.4 3.4 reshape.294
  77.8 4.3 fusion.12
  82.2 55.8 %all-reduce.4.cloned.1.call-done = f32[2,256,256]{1,2,0:T(8,128)} async-done(((f32[2,256,256]{1,2,0:T(8,128)}), f32[2,256,256]{1,2,0:T(8,128)}) %all-reduce.4.cloned.1.call-update) | async-done | bytes 524304 | tf_op jit(solution)/shard_map/psum | solution.py:61
  138.0 17.2 %copy.123 = f32[2,256,256]{0,2,1:T(8,128)} copy(f32[2,256,256]{1,2,0:T(8,128)} %all-reduce.4.cloned.1.call-done) | data formatting | bytes 1048576 | tf_op jit(solution)/shard_map/psum | solution.py:61
  155.2 2.3 gather_fusion.4
  159.8 23.5 %custom-call.23 = f32[2,128,128]{2,1,0:T(8,128)S(1)} custom-call(f32[2,128,128]{2,1,0:T(8,128)S(1)} %cholesky.198), custom_call_target="Cholesky" | custom-call | tf_op jit(solution)/shard_map/vmap(jit(cholesky))/cholesky | solution.py:30
  183.4 20.2 %custom-call.24 = f32[2,1,128,128]{2,3,1,0:T(8,128)S(1)} custom-call(f32[2,1,128,128]{3,2,1,0:T(8,128)S(1)} %select_bitcast_fusion.1), custom_call_target="InvertDiagBlocksLowerTriangular" | custom-call | tf_op jit(solution)/shard_map/vmap(jit(cholesky))/cholesky | solution.py:30
  203.6 1.2 constant_dynamic-update-slice_fusion.3
  204.8 1.3 convolution_subtract_fusion.5
  206.1 23.5 %custom-call.25 = f32[2,128,128]{2,1,0:T(8,128)S(1)} custom-call(f32[2,128,128]{2,1,0:T(8,128)S(1)} %convolution_subtract_fusion.5), custom_call_target="Cholesky" | custom-call | tf_op jit(solution)/shard_map/vmap(jit(cholesky))/cholesky | solution.py:30
  230.1 4.1 while.4
  230.7 1.4 bitcast_dynamic-update-slice_fusion.4
  232.7 1.4 bitcast_dynamic-update-slice_fusion.4
  234.2 39.5 %custom-call.26 = f32[2,2,128,128]{2,3,1,0:T(8,128)S(1)} custom-call(f32[2,2,128,128]{3,2,1,0:T(8,128)S(1)} %bitcast.143), custom_call_target="InvertDiagBlocksLowerTriangular" | custom-call | tf_op jit(solution)/shard_map/vmap(jit(_cho_solve))/triangular_solve | solution.py:31
  273.7 2.7 fusion.42
  278.9 4.9 fusion.10
  283.8 2.0 copy.139
  285.8 2.2 convolution_bitcast_fusion
  288.0 1.5 copy.140
  289.4 4.6 all-to-all-start.1
  295.4 43.1 %all-to-all-done.1 = f32[1024,4,128]{2,0,1:T(8,128)} async-done(((f32[1024,4,128]{2,0,1:T(8,128)}), f32[1024,4,128]{2,0,1:T(8,128)}, u32[]{:S(2)}, u32[]{:S(2)}) %all-to-all-start.1) | async-done | bytes 2097184 | tf_op jit(solution)/shard_map/all_to_all | solution.py:57
  338.5 6.1 %fusion.20 = f32[1024,4,128]{2,1,0:T(4,128)} fusion(f32[1024,4,128]{2,0,1:T(8,128)} %all-to-all-done.1, s32[4]{0:T(128)S(1)} %and_select_fusion), kind=kOutput, calls=%fused_computation.30 | convolution fusion | flops 25165840 | bytes 4194320 | tf_op jit(solution)/shard_map/sd,rdw->rsw/dot_general | solution.py:59
  344.7 3.3 reshape.296
  348.0 4.3 fusion.8
  352.3 55.1 %all-reduce.6.cloned.1.call-done = f32[2,256,256]{1,2,0:T(8,128)} async-done(((f32[2,256,256]{1,2,0:T(8,128)}), f32[2,256,256]{1,2,0:T(8,128)}) %all-reduce.6.cloned.1.call-update) | async-done | bytes 524304 | tf_op jit(solution)/shard_map/psum | solution.py:61
  407.4 17.2 %copy.145 = f32[2,256,256]{0,2,1:T(8,128)} copy(f32[2,256,256]{1,2,0:T(8,128)} %all-reduce.6.cloned.1.call-done) | data formatting | bytes 1048576 | tf_op jit(solution)/shard_map/psum | solution.py:61
  424.6 2.3 gather_fusion.9
  429.3 23.5 %custom-call.27 = f32[2,128,128]{2,1,0:T(8,128)S(1)} custom-call(f32[2,128,128]{2,1,0:T(8,128)S(1)} %cholesky.201), custom_call_target="Cholesky" | custom-call | tf_op jit(solution)/shard_map/vmap(jit(cholesky))/cholesky | solution.py:30
  452.8 20.1 %custom-call.28 = f32[2,1,128,128]{2,3,1,0:T(8,128)S(1)} custom-call(f32[2,1,128,128]{3,2,1,0:T(8,128)S(1)} %select_bitcast_fusion), custom_call_target="InvertDiagBlocksLowerTriangular" | custom-call | tf_op jit(solution)/shard_map/vmap(jit(cholesky))/cholesky | solution.py:30
  472.9 1.2 constant_dynamic-update-slice_fusion.1
  474.1 1.3 convolution_subtract_fusion.4
  475.4 23.5 %custom-call.29 = f32[2,128,128]{2,1,0:T(8,128)S(1)} custom-call(f32[2,128,128]{2,1,0:T(8,128)S(1)} %convolution_subtract_fusion.4), custom_call_target="Cholesky" | custom-call | tf_op jit(solution)/shard_map/vmap(jit(cholesky))/cholesky | solution.py:30
  499.3 4.1 while.5
  499.9 1.4 bitcast_dynamic-update-slice_fusion.5
  502.0 1.4 bitcast_dynamic-update-slice_fusion.5
  503.4 39.5 %custom-call.30 = f32[2,2,128,128]{2,3,1,0:T(8,128)S(1)} custom-call(f32[2,2,128,128]{3,2,1,0:T(8,128)S(1)} %bitcast.142), custom_call_target="InvertDiagBlocksLowerTriangular" | custom-call | tf_op jit(solution)/shard_map/vmap(jit(_cho_solve))/triangular_solve | solution.py:31
  543.0 2.7 fusion.40
  548.1 4.9 fusion.6
  553.0 2.9 copy.161
  (95 shorter events, 19.1 us)
Async XLA Ops:
  9.9 4.5 copy-start.4
  20.0 6.0 %copy-start.5 = (s32[2,16]{1,0:T(2,128)S(1)}, s32[2,16]{1,0:T(2,128)}, u32[]{:S(2)}) copy-start(s32[2,16]{1,0:T(2,128)} %param.8) | copy-start | bytes 388
  20.0 49.9 %all-to-all-start = ((f32[1024,4,128]{2,0,1:T(8,128)}), f32[1024,4,128]{2,0,1:T(8,128)S(1)}, u32[]{:S(2)}, u32[]{:S(2)}) async-start(f32[1024,4,128]{2,0,1:T(8,128)} %copy.118), calls=%async_computation | async-start | bytes 4194304 | tf_op jit(solution)/shard_map/all_to_all | solution.py:57
  24.6 113.4 %all-reduce.4.cloned.1.call-start = ((), (), s32[]{:S(2)}) async-start(), calls=%async_computation.2 | async-start | bytes 1048576 | tf_op jit(solution)/shard_map/psum | solution.py:61
  138.0 19.6 %copy-start.3 = (f32[2,256,256]{1,2,0:T(8,128)S(1)}, f32[2,256,256]{1,2,0:T(8,128)}, u32[]{:S(2)}) copy-start(f32[2,256,256]{1,2,0:T(8,128)} %all-reduce.4.cloned.1.call-done) | copy-start | bytes 1572868
  159.0 0.8 copy-start.1
  289.4 49.1 %all-to-all-start.1 = ((f32[1024,4,128]{2,0,1:T(8,128)}), f32[1024,4,128]{2,0,1:T(8,128)}, u32[]{:S(2)}, u32[]{:S(2)}) async-start(f32[1024,4,128]{2,0,1:T(8,128)} %copy.140), calls=%async_computation.1 | async-start | bytes 4194304 | tf_op jit(solution)/shard_map/all_to_all | solution.py:57
  294.1 113.4 %all-reduce.6.cloned.1.call-start = ((), (), s32[]{:S(2)}) async-start(), calls=%async_computation.3 | async-start | bytes 1048576 | tf_op jit(solution)/shard_map/psum | solution.py:61
  407.4 19.6 %copy-start.2 = (f32[2,256,256]{1,2,0:T(8,128)S(1)}, f32[2,256,256]{1,2,0:T(8,128)}, u32[]{:S(2)}) copy-start(f32[2,256,256]{1,2,0:T(8,128)} %all-reduce.6.cloned.1.call-done) | copy-start | bytes 1572868
  428.5 0.8 copy-start
Sparse Core Ops, SparseCore 0:
  82.3 55.7 all-reduce.3
  352.4 54.9 all-reduce.5
where the time goes:
time: 572 us; the launch traced here: 563 us
  other arithmetic  218 us (38%)
  waiting for transfers between devices  197 us (34%)
  local copies, waits for them, and re-layouts  72 us (13%)
  matrix products  52.7 us (9%)
  between operations  14.1 us (2%)
  starting transfers between devices  9.28 us (2%)
    another operation x18, other arithmetic, cayley(): lower_factor = jnp.linalg.cholesky(definite)  135 us
    psum x2, waiting for transfers between devices, on_device(): gram_matrix = lax.psum(local_gram(paired, paired), 'row')  111 us
    all_to_all x2, waiting for transfers between devices, on_device(): lax.all_to_all(outgoing, 'col', split_axis=1, concat_axis=1, tiled=True)  85.7 us
    another operation x6, other arithmetic, cayley(): return jax.scipy.linalg.cho_solve((lower_factor, True), numerator)  79.3 us
    psum x2, local copies, waits for them, and re-layouts, on_device(): gram_matrix = lax.psum(local_gram(paired, paired), 'row')  34.4 us
  transfers between devices with their start and end apart: 4, of which 4 were waited for; matrix products, arithmetic and copies ran while one was open for 1% of the time, Pallas kernels for 0%

commit v1 on v0

v1 whole, which is shorter than its diff:
```python
import functools

import jax
import jax.numpy as jnp
from jax import lax
from jax.experimental import pallas as pl
from jax.experimental.pallas import tpu as pltpu
from jax.sharding import PartitionSpec as P

W = 128
RB = 128
ROUNDS = 2
CHUNKS = 4
SCALED_STEPS = 7
TRUE_STEPS = 2
DAMPING = 0.01
F32 = jnp.float32
BF16 = jnp.bfloat16
MESH = pl.DeviceIdType.MESH


def split(x):
    high = x.astype(BF16)
    return high, (x - high.astype(F32)).astype(BF16)


def dot(a, b):
    return jnp.dot(a, b, preferred_element_type=F32)


def dot3(a, b):
    a_high, a_low = split(a)
    b_high, b_low = split(b)
    return dot(a_high, b_high) + (dot(a_high, b_low) + dot(a_low, b_high))


def dot_t(a, b):
    return lax.dot_general(a, b, (((0,), (0,)), ((), ())), preferred_element_type=F32)


def rotation(gram, eye, stack):
    size = gram.shape[0]
    on_diagonal = gram * eye
    diag_rows = jnp.sum(on_diagonal, axis=1, keepdims=True)
    diag_cols = jnp.sum(on_diagonal, axis=0, keepdims=True)
    spread = diag_rows - diag_cols
    joined = diag_rows + diag_cols
    half = 0.5 * gram * spread / (spread * spread + gram * gram + DAMPING * joined * joined)
    squared = dot3(half, half)
    total = jnp.sum(jnp.sum(squared * squared, axis=1, keepdims=True), axis=0, keepdims=True)
    upper = 1.0 + 1.001 * jnp.sqrt(0.5 * total)
    stack[:size] = eye - squared
    stack[size:] = eye - half

    def scaled(_, bounds):
        low, high = bounds
        scale = 2.0 / (low + high)
        delta = (high - low) / (high + low)
        factor = (2.0 * scale) * eye - (scale * scale) * stack[:size]
        stack[...] = dot3(stack[...], factor)
        return 1.0 - delta * delta, jnp.ones_like(high)

    lax.fori_loop(0, SCALED_STEPS, scaled, (jnp.ones_like(upper), upper))

    def true(_, carry):
        inverse = stack[size:]
        residual = (eye - inverse) - dot3(half, inverse)
        stack[size:] = inverse + dot3(inverse, residual)
        return carry

    lax.fori_loop(0, TRUE_STEPS, true, 0)
    return 2.0 * stack[size:] - eye


def kernel(
    groups, members, factor_ref, support_ref, plan_ref, out_ref,
    cur, send, recv, gram, gram_in, rot, rot_pair, stack,
    move_send, move_recv, swap_send, swap_recv, sum_send, sum_recv, rot_send, rot_recv,
):
    slots, rows, _ = cur.shape
    size = 2 * W
    chunk = rows // CHUNKS
    chips = members // 2
    stages = chips.bit_length() - 1
    g = lax.axis_index("col")
    m = lax.axis_index("row")
    core = lax.rem(m, 2)
    chip = m // 2
    partner = m + 1 - 2 * core

    def flipped(bit):
        step = 1 << bit
        on = lax.rem(chip // step, 2)
        return (chip + step - 2 * step * on) * 2 + core

    peers = [{"col": lax.rem(g + o, groups), "row": m} for o in range(1, groups)]
    peers += [{"col": g, "row": partner}]
    peers += [{"col": g, "row": flipped(b)} for b in range(stages)]
    barrier = pltpu.get_barrier_semaphore()
    for peer in peers:
        pl.semaphore_signal(barrier, inc=1, device_id=peer, device_id_type=MESH)

    row_ids = lax.broadcasted_iota(jnp.int32, (size, size), 0)
    col_ids = lax.broadcasted_iota(jnp.int32, (size, size), 1)
    eye = (row_ids == col_ids).astype(F32)

    for s in range(slots):
        for b in range(rows // RB):
            span = pl.ds(b * RB, RB)
            weight = support_ref[g * slots + s, b].astype(F32)
            cur[s, span] = factor_ref[span, s * W:(s + 1) * W] * weight

    def before(r, position):
        return position if r == 0 else plan_ref[r - 1, position]

    blocks = groups * slots
    pick, take = [], []
    for r in range(ROUNDS):
        dest = []
        for s in range(slots):
            block = before(r, g * slots + s)
            dest.append(sum(
                jnp.where(plan_ref[r, j] == block, j // slots, 0) for j in range(blocks)))
        pick.append([
            jnp.minimum(slots - 1, sum(
                jnp.where(dest[s] == lax.rem(g + o, groups), s, 0) for s in range(slots)))
            for o in range(groups)])
        take.append([])
        for s in range(slots):
            block = plan_ref[r, g * slots + s]
            take[r].append(jnp.minimum(groups - 1, sum(
                jnp.where(before(r, j) == block, j // slots, 0) for j in range(blocks))))

    pl.semaphore_wait(barrier, len(peers))

    copies = []

    def start(copy):
        copy.start()
        copies.append(copy)
        return copy

    def dispatch(r, q):
        span = pl.ds(q * chunk, chunk)
        out = []
        for o in range(1, groups):
            send[r, o - 1, span] = cur[pick[r][o], span]
            out.append(start(pltpu.make_async_remote_copy(
                src_ref=send.at[r, o - 1, span],
                dst_ref=recv[r][q].at[g],
                send_sem=move_send.at[r, q, o - 1],
                recv_sem=move_recv.at[r, q, o - 1],
                device_id=peers[o - 1],
                device_id_type=MESH,
            )))
        recv[r][q][g] = cur[pick[r][0], span]
        return out

    def load_pair(r, k, q):
        held = recv[r][q]
        return jnp.concatenate([held[take[r][2 * k]], held[take[r][2 * k + 1]]], axis=1)

    moves = [dispatch(0, q) for q in range(CHUNKS)]
    for r in range(ROUNDS):
        for q in range(CHUNKS):
            for copy in moves[q]:
                copy.wait_recv()
            for k in range(2):
                high, low = split(load_pair(r, k, q))
                mixed = dot_t(high, low)
                part = dot_t(high, high) + (mixed + mixed.T)
                gram_in[r, k] = part if q == 0 else gram_in[r, k] + part
        swap = start(pltpu.make_async_remote_copy(
            src_ref=gram_in.at[r, 1 - core],
            dst_ref=gram_in.at[r, 2],
            send_sem=swap_send.at[r],
            recv_sem=swap_recv.at[r],
            device_id=peers[groups - 1],
            device_id_type=MESH,
        ))
        swap.wait_recv()
        total = gram_in[r, core] + gram_in[r, 2]
        for stage in range(stages):
            gram[r, 2 * stage] = total
            pair = []
            for h in range(2):
                bit = (stage + h * (stages // 2)) % stages
                part = pl.ds(h * W, W)
                pair.append(start(pltpu.make_async_remote_copy(
                    src_ref=gram.at[r, 2 * stage, part],
                    dst_ref=gram.at[r, 2 * stage + 1, part],
                    send_sem=sum_send.at[r, stage, h],
                    recv_sem=sum_recv.at[r, stage, h],
                    device_id=peers[groups + bit],
                    device_id_type=MESH,
                )))
            for copy in pair:
                copy.wait_recv()
            total = total + gram[r, 2 * stage + 1]
        rot[r, 0] = rotation(total, eye, stack)
        back = start(pltpu.make_async_remote_copy(
            src_ref=rot.at[r, 0],
            dst_ref=rot.at[r, 1],
            send_sem=rot_send.at[r],
            recv_sem=rot_recv.at[r],
            device_id=peers[groups - 1],
            device_id_type=MESH,
        ))
        back.wait_recv()
        rot_pair[core] = rot[r, 0]
        rot_pair[1 - core] = rot[r, 1]
        moves = []
        for q in range(CHUNKS):
            span = pl.ds(q * chunk, chunk)
            for k in range(2):
                turned = dot3(load_pair(r, k, q), rot_pair[k])
                if r == ROUNDS - 1:
                    out_ref[span, k * size:(k + 1) * size] = turned
                else:
                    cur[2 * k, span] = turned[:, :W]
                    cur[2 * k + 1, span] = turned[:, W:]
            if r < ROUNDS - 1:
                moves.append(dispatch(r + 1, q))
    for copy in copies:
        copy.wait_send()


def on_device(groups, members, factor, support, plan):
    rows = factor.shape[0]
    slots = factor.shape[1] // W
    chips = members // 2
    stages = chips.bit_length() - 1
    assert slots == 4 and chips == 1 << stages and stages >= 1
    size = 2 * W
    dma = pltpu.SemaphoreType.DMA
    vmem = pl.BlockSpec(memory_space=pltpu.VMEM)
    smem = pl.BlockSpec(memory_space=pltpu.SMEM)
    return pl.pallas_call(
        functools.partial(kernel, groups, members),
        out_shape=jax.ShapeDtypeStruct(factor.shape, F32),
        in_specs=[vmem, smem, smem],
        out_specs=vmem,
        scratch_shapes=[
            pltpu.VMEM((slots, rows, W), F32),
            pltpu.VMEM((ROUNDS, groups - 1, rows, W), F32),
            [[pltpu.VMEM((groups, rows // CHUNKS, W), F32)] * CHUNKS] * ROUNDS,
            pltpu.VMEM((ROUNDS, 2 * stages, size, size), F32),
            pltpu.VMEM((ROUNDS, 3, size, size), F32),
            pltpu.VMEM((ROUNDS, 2, size, size), F32),
            pltpu.VMEM((2, size, size), F32),
            pltpu.VMEM((2 * size, size), F32),
            dma((ROUNDS, CHUNKS, groups - 1)),
            dma((ROUNDS, CHUNKS, groups - 1)),
            dma((ROUNDS,)),
            dma((ROUNDS,)),
            dma((ROUNDS, stages, 2)),
            dma((ROUNDS, stages, 2)),
            dma((ROUNDS,)),
            dma((ROUNDS,)),
        ],
        compiler_params=pltpu.CompilerParams(
            collective_id=0, has_side_effects=True, vmem_limit_bytes=48 * 1024 * 1024
        ),
    )(factor, support, plan)


def solution(mesh):
    return jax.shard_map(
        functools.partial(on_device, mesh.shape["col"], mesh.shape["row"]),
        mesh=mesh,
        in_specs=(P("row", "col"), P(None, "row"), P()),
        out_specs=P("row", "col"),
        check_vma=False,
    )
```

time: 572 us -> 138 us (0.24); the launches traced: 563 us -> 138 us
  other arithmetic: 218 us -> 0 us
  waiting for transfers between devices: 197 us -> 0 us
  Pallas kernels: 0 us -> 134 us
  local copies, waits for them, and re-layouts: 72 us -> 4.35 us
  matrix products: 52.7 us -> 0 us
  between operations: 14.1 us -> 0.01 us
  starting transfers between devices: 9.28 us -> 0 us
    another operation x24 -> x0, other arithmetic: 214 us -> none  [the longest x18 135 us: cayley(): lower_factor = jnp.linalg.cholesky(definite)]
    pallas_call x0 -> x1, Pallas kernels: none -> 134 us  [on_device(): pl.pallas_call(functools.partial(kernel, groups, members), out_shape=jax....]
    psum x2 -> x0, waiting for transfers between devices: 111 us -> none  [on_device(): gram_matrix = lax.psum(local_gram(paired, paired), 'row')]
    all_to_all x2 -> x0, waiting for transfers between devices: 85.7 us -> none  [on_device(): lax.all_to_all(outgoing, 'col', split_axis=1, concat_axis=1, tiled=True)]
    dot_general x12 -> x0, matrix products: 43 us -> none  [the longest x2 10.7 us: on_device(): arranged = jnp.einsum('sd,rdw->rsw', take_pick, incoming, precision=precise)]
    psum x2 -> x0, local copies, waits for them, and re-layouts: 34.4 us -> none  [on_device(): gram_matrix = lax.psum(local_gram(paired, paired), 'row')]
    another operation x20 -> x0, local copies, waits for them, and re-layouts: 11.2 us -> none  [the longest x15 8.28 us: cayley(): return jax.scipy.linalg.cho_solve((lower_factor, True), numerator)]
    reshape x4 -> x0, local copies, waits for them, and re-layouts: 10.7 us -> none  [the longest x2 6.7 us: on_device(): paired = arranged.reshape(rows_here, pair_count, 2 * W)]
  transfers between devices with their start and end apart: 4 -> 0, of which waited for: 4 -> 0; matrix products, arithmetic and copies ran while one was open for 1% -> 0% of each run, Pallas kernels for 0% -> 0%
where the time goes in v1:
time: 138 us
  Pallas kernels  134 us (97%)
  local copies, waits for them, and re-layouts  4.35 us (3%)
    pallas_call x1, Pallas kernels, on_device(): pl.pallas_call(functools.partial(kernel, groups, members), out_shape=jax....  134 us
    unnamed x6, local copies, waits for them, and re-layouts  4.35 us

profile of v1, /device:TPU:25, one launch (start us, length us, event | category | flops | bytes accessed | tf_op | source)
XLA Modules:
  0.0 137.9 jit_solution(5884639294468071140)
XLA Ops:
  0.0 0.8 copy.4.support_ref
  0.8 0.0 copy-start
  0.8 1.6 %copy-done = f32[1024,512]{1,0:T(8,128)S(1)} copy-done((f32[1024,512]{1,0:T(8,128)S(1)}, f32[1024,512]{1,0:T(8,128)}, u32[]{:S(2)}) %copy-start) | copy-done | bytes 2097176
  2.3 0.0 copy-start.1
  2.4 0.7 copy-done.1
  3.0 133.6 %shard_map.37 = f32[1024,512]{1,0:T(8,128)S(1)} custom-call(f32[1024,512]{1,0:T(8,128)S(1)} %copy-done, s32[16,8]{1,0:T(8,128)S(1)} %copy.4.support_ref, s32[2,16]{1,0:T(2,128)S(1)} %copy-done.1), custom_call_target="tpu_custom_call" | custom-call | tf_op jit(solution)/shard_map/pallas_call | solution.py:238
  136.6 1.3 copy.6
Async XLA Ops:
  0.8 1.6 %copy-start = (f32[1024,512]{1,0:T(8,128)S(1)}, f32[1024,512]{1,0:T(8,128)}, u32[]{:S(2)}) copy-start(f32[1024,512]{1,0:T(8,128)} %factor_ref.1) | copy-start | bytes 6291460
  2.3 0.7 copy-start.1

commit v2 on v1

--- a/solution.py
+++ b/solution.py
@@ -72,10 +72,31 @@
     return 2.0 * stack[size:] - eye
 
 
+def pack(gram):
+    first, last = gram[:W, :W], gram[W:, W:]
+    row_ids = lax.broadcasted_iota(jnp.int32, (W, W), 0)
+    col_ids = lax.broadcasted_iota(jnp.int32, (W, W), 1)
+    tile = jnp.where(row_ids >= col_ids, first, last)
+    diagonal = jnp.sum(jnp.where(row_ids == col_ids, last, 0.0), axis=0, keepdims=True)
+    return gram[:W, W:], tile, jnp.broadcast_to(diagonal, (8, W))
+
+
+def unpack(packed):
+    cross, tile, diagonal = packed[:W], packed[W:2 * W], packed[2 * W:2 * W + 1]
+    row_ids = lax.broadcasted_iota(jnp.int32, (W, W), 0)
+    col_ids = lax.broadcasted_iota(jnp.int32, (W, W), 1)
+    lower = jnp.where(row_ids > col_ids, tile, 0.0)
+    upper = jnp.where(row_ids < col_ids, tile, 0.0)
+    first = lower + lower.T + jnp.where(row_ids == col_ids, tile, 0.0)
+    last = upper + upper.T + jnp.where(row_ids == col_ids, diagonal, 0.0)
+    top = jnp.concatenate([first, cross], axis=1)
+    return jnp.concatenate([top, jnp.concatenate([cross.T, last], axis=1)], axis=0)
+
+
 def kernel(
     groups, members, factor_ref, support_ref, plan_ref, out_ref,
-    cur, send, recv, gram, gram_in, rot, rot_pair, stack,
-    move_send, move_recv, swap_send, swap_recv, sum_send, sum_recv, rot_send, rot_recv,
+    held, cur, send, recv, acc, gram, gram_in, rot, rot_pair, stack,
+    load_sem, move_send, move_recv, swap_send, swap_recv, sum_send, sum_recv, rot_send, rot_recv,
 ):
     slots, rows, _ = cur.shape
     size = 2 * W
@@ -93,6 +114,12 @@
         on = lax.rem(chip // step, 2)
         return (chip + step - 2 * step * on) * 2 + core
 
+    loads = []
+    for q in range(CHUNKS):
+        span = pl.ds(q * chunk, chunk)
+        loads.append(pltpu.make_async_copy(factor_ref.at[span], held.at[span], load_sem.at[q]))
+        loads[q].start()
+
     peers = [{"col": lax.rem(g + o, groups), "row": m} for o in range(1, groups)]
     peers += [{"col": g, "row": partner}]
     peers += [{"col": g, "row": flipped(b)} for b in range(stages)]
@@ -104,11 +131,13 @@
     col_ids = lax.broadcasted_iota(jnp.int32, (size, size), 1)
     eye = (row_ids == col_ids).astype(F32)
 
-    for s in range(slots):
-        for b in range(rows // RB):
-            span = pl.ds(b * RB, RB)
-            weight = support_ref[g * slots + s, b].astype(F32)
-            cur[s, span] = factor_ref[span, s * W:(s + 1) * W] * weight
+    def mask(q):
+        loads[q].wait()
+        for s in range(slots):
+            for b in range(q * chunk // RB, (q + 1) * chunk // RB):
+                span = pl.ds(b * RB, RB)
+                weight = support_ref[b, g * slots + s].astype(F32)
+                cur[s, span] = held[span, s * W:(s + 1) * W] * weight
 
     def before(r, position):
         return position if r == 0 else plan_ref[r - 1, position]
@@ -133,7 +162,7 @@
 
     pl.semaphore_wait(barrier, len(peers))
 
-    copies = []
+    copies, stores = [], []
 
     def start(copy):
         copy.start()
@@ -160,7 +189,10 @@
         held = recv[r][q]
         return jnp.concatenate([held[take[r][2 * k]], held[take[r][2 * k + 1]]], axis=1)
 
-    moves = [dispatch(0, q) for q in range(CHUNKS)]
+    moves = []
+    for q in range(CHUNKS):
+        mask(q)
+        moves.append(dispatch(0, q))
     for r in range(ROUNDS):
         for q in range(CHUNKS):
             for copy in moves[q]:
@@ -169,7 +201,12 @@
                 high, low = split(load_pair(r, k, q))
                 mixed = dot_t(high, low)
                 part = dot_t(high, high) + (mixed + mixed.T)
-                gram_in[r, k] = part if q == 0 else gram_in[r, k] + part
+                acc[k] = part if q == 0 else acc[k] + part
+        for k in range(2):
+            cross, tile, diagonal = pack(acc[k])
+            gram_in[r, k, :W] = cross
+            gram_in[r, k, W:size] = tile
+            gram_in[r, k, size:] = diagonal
         swap = start(pltpu.make_async_remote_copy(
             src_ref=gram_in.at[r, 1 - core],
             dst_ref=gram_in.at[r, 2],
@@ -185,7 +222,7 @@
             pair = []
             for h in range(2):
                 bit = (stage + h * (stages // 2)) % stages
-                part = pl.ds(h * W, W)
+                part = pl.ds(0, W) if h == 0 else pl.ds(W, W + 8)
                 pair.append(start(pltpu.make_async_remote_copy(
                     src_ref=gram.at[r, 2 * stage, part],
                     dst_ref=gram.at[r, 2 * stage + 1, part],
@@ -197,7 +234,7 @@
             for copy in pair:
                 copy.wait_recv()
             total = total + gram[r, 2 * stage + 1]
-        rot[r, 0] = rotation(total, eye, stack)
+        rot[r, 0] = rotation(unpack(total), eye, stack)
         back = start(pltpu.make_async_remote_copy(
             src_ref=rot.at[r, 0],
             dst_ref=rot.at[r, 1],
@@ -215,14 +252,19 @@
             for k in range(2):
                 turned = dot3(load_pair(r, k, q), rot_pair[k])
                 if r == ROUNDS - 1:
-                    out_ref[span, k * size:(k + 1) * size] = turned
+                    held[span, k * size:(k + 1) * size] = turned
                 else:
                     cur[2 * k, span] = turned[:, :W]
                     cur[2 * k + 1, span] = turned[:, W:]
-            if r < ROUNDS - 1:
+            if r == ROUNDS - 1:
+                stores.append(pltpu.make_async_copy(held.at[span], out_ref.at[span], load_sem.at[q]))
+                stores[q].start()
+            else:
                 moves.append(dispatch(r + 1, q))
     for copy in copies:
         copy.wait_send()
+    for copy in stores:
+        copy.wait()
 
 
 def on_device(groups, members, factor, support, plan):
@@ -233,22 +275,24 @@
     assert slots == 4 and chips == 1 << stages and stages >= 1
     size = 2 * W
     dma = pltpu.SemaphoreType.DMA
-    vmem = pl.BlockSpec(memory_space=pltpu.VMEM)
     smem = pl.BlockSpec(memory_space=pltpu.SMEM)
     return pl.pallas_call(
         functools.partial(kernel, groups, members),
         out_shape=jax.ShapeDtypeStruct(factor.shape, F32),
-        in_specs=[vmem, smem, smem],
-        out_specs=vmem,
+        in_specs=[pl.BlockSpec(memory_space=pl.ANY), smem, smem],
+        out_specs=pl.BlockSpec(memory_space=pl.ANY),
         scratch_shapes=[
+            pltpu.VMEM(factor.shape, F32),
             pltpu.VMEM((slots, rows, W), F32),
             pltpu.VMEM((ROUNDS, groups - 1, rows, W), F32),
             [[pltpu.VMEM((groups, rows // CHUNKS, W), F32)] * CHUNKS] * ROUNDS,
-            pltpu.VMEM((ROUNDS, 2 * stages, size, size), F32),
-            pltpu.VMEM((ROUNDS, 3, size, size), F32),
+            pltpu.VMEM((2, size, size), F32),
+            pltpu.VMEM((ROUNDS, 2 * stages, size + 8, W), F32),
+            pltpu.VMEM((ROUNDS, 3, size + 8, W), F32),
             pltpu.VMEM((ROUNDS, 2, size, size), F32),
             pltpu.VMEM((2, size, size), F32),
             pltpu.VMEM((2 * size, size), F32),
+            dma((CHUNKS,)),
             dma((ROUNDS, CHUNKS, groups - 1)),
             dma((ROUNDS, CHUNKS, groups - 1)),
             dma((ROUNDS,)),
@@ -259,9 +303,9 @@
             dma((ROUNDS,)),
         ],
         compiler_params=pltpu.CompilerParams(
-            collective_id=0, has_side_effects=True, vmem_limit_bytes=48 * 1024 * 1024
+            collective_id=0, has_side_effects=True, vmem_limit_bytes=123 * 512 * 1024
         ),
-    )(factor, support, plan)
+    )(factor, support.T, plan)
 
 
 def solution(mesh):

time: 138 us -> 132 us (0.957)
  Pallas kernels: 134 us -> 129 us
    pallas_call x1, Pallas kernels: 134 us -> 129 us  [on_device(): pl.pallas_call(functools.partial(kernel, groups, members), out_shape=jax....]
    unnamed x6 -> x1, local copies, waits for them, and re-layouts: 4.35 us -> 3.08 us
where the time goes in v2:
time: 132 us
  Pallas kernels  129 us (98%)
  local copies, waits for them, and re-layouts  3.08 us (2%)
    pallas_call x1, Pallas kernels, on_device(): pl.pallas_call(functools.partial(kernel, groups, members), out_shape=jax....  129 us
    unnamed x1, local copies, waits for them, and re-layouts  3.08 us

profile of v2, /device:TPU:25, one launch (start us, length us, event | category | flops | bytes accessed | tf_op | source)
XLA Modules:
  0.0 132.1 jit_solution(5586125738092493359)
XLA Ops:
  0.0 129.0 %shard_map.37 = f32[1024,512]{1,0:T(8,128)} custom-call(f32[1024,512]{1,0:T(8,128)} %factor_ref.1, s32[8,16]{1,0:T(8,128)} %bitcast.1, s32[2,16]{1,0:T(2,128)} %plan_ref.1), custom_call_target="tpu_custom_call" | custom-call | tf_op jit(solution)/shard_map/pallas_call | solution.py:279
  129.0 3.1 %copy.5 = f32[1024,512]{1,0:T(8,128)} copy(f32[1024,512]{1,0:T(8,128)} %shard_map.37) | data formatting | bytes 4194304

commit v3 on v2

--- a/solution.py
+++ b/solution.py
@@ -95,8 +95,10 @@
 
 def kernel(
     groups, members, factor_ref, support_ref, plan_ref, out_ref,
-    held, cur, send, recv, acc, gram, gram_in, rot, rot_pair, stack,
-    load_sem, move_send, move_recv, swap_send, swap_recv, sum_send, sum_recv, rot_send, rot_recv,
+    held, cur, send, recv, early_out, early_in, turn_out, turns,
+    acc, gram, gram_in, rot, rot_pair, stack,
+    load_sem, move_send, move_recv, early_send, early_recv, turn_send, turn_recv, spread_send, spread_recv,
+    swap_send, swap_recv, sum_send, sum_recv, rot_send, rot_recv,
 ):
     slots, rows, _ = cur.shape
     size = 2 * W
@@ -189,6 +191,60 @@
         held = recv[r][q]
         return jnp.concatenate([held[take[r][2 * k]], held[take[r][2 * k + 1]]], axis=1)
 
+    def stage_early():
+        for o in range(1, groups):
+            second = pick[1][o] // 2 == 1
+            left = jnp.where(second, take[0][2], take[0][0])
+            right = jnp.where(second, take[0][3], take[0][1])
+            early_out[o - 1, :, :W] = recv[0][0][left]
+            early_out[o - 1, :, W:] = recv[0][0][right]
+
+    def send_early():
+        return [start(pltpu.make_async_remote_copy(
+            src_ref=early_out.at[o - 1],
+            dst_ref=early_in.at[o - 1],
+            send_sem=early_send.at[o - 1],
+            recv_sem=early_recv.at[o - 1],
+            device_id=peers[o - 1],
+            device_id_type=MESH,
+        )) for o in range(1, groups)]
+
+    share = size // members
+    mine = pl.ds(pl.multiple_of(m * share, share), share)
+
+    def send_turns():
+        out = []
+        for o in range(1, groups):
+            wide = rot_pair[pick[1][o] // 2, mine]
+            turn_out[o - 1] = jnp.where(lax.rem(pick[1][o], 2) == 0, wide[:, :W], wide[:, W:])
+            out.append(start(pltpu.make_async_remote_copy(
+                src_ref=turn_out.at[o - 1],
+                dst_ref=turns.at[o - 1, mine],
+                send_sem=turn_send.at[o - 1],
+                recv_sem=turn_recv.at[o - 1],
+                device_id=peers[o - 1],
+                device_id_type=MESH,
+            )))
+        return out
+
+    def finish_early(turned, early):
+        for copy in turned:
+            copy.wait_recv()
+        for b in range(stages + 1):
+            span = pl.ds(pl.multiple_of((m // (1 << b)) * (1 << b) * share, share), share << b)
+            start(pltpu.make_async_remote_copy(
+                src_ref=turns.at[:, span],
+                dst_ref=turns.at[:, span],
+                send_sem=spread_send.at[b],
+                recv_sem=spread_recv.at[b],
+                device_id=peers[groups - 1 + b],
+                device_id_type=MESH,
+            )).wait_recv()
+        for o in range(1, groups):
+            early[o - 1].wait_recv()
+            source = lax.rem(g + groups - o, groups)
+            recv[1][0][source] = dot3(early_in[o - 1], turns[o - 1])
+
     moves = []
     for q in range(CHUNKS):
         mask(q)
@@ -197,11 +253,15 @@
         for q in range(CHUNKS):
             for copy in moves[q]:
                 copy.wait_recv()
+            if r == 0 and q == CHUNKS - 1:
+                early = send_early()
             for k in range(2):
                 high, low = split(load_pair(r, k, q))
                 mixed = dot_t(high, low)
                 part = dot_t(high, high) + (mixed + mixed.T)
                 acc[k] = part if q == 0 else acc[k] + part
+            if r == 0 and q == 0:
+                stage_early()
         for k in range(2):
             cross, tile, diagonal = pack(acc[k])
             gram_in[r, k, :W] = cross
@@ -247,7 +307,9 @@
         rot_pair[core] = rot[r, 0]
         rot_pair[1 - core] = rot[r, 1]
         moves = []
-        for q in range(CHUNKS):
+        if r < ROUNDS - 1:
+            turned_copies = send_turns()
+        for q in (range(CHUNKS) if r == ROUNDS - 1 else [*range(1, CHUNKS), 0]):
             span = pl.ds(q * chunk, chunk)
             for k in range(2):
                 turned = dot3(load_pair(r, k, q), rot_pair[k])
@@ -259,8 +321,12 @@
             if r == ROUNDS - 1:
                 stores.append(pltpu.make_async_copy(held.at[span], out_ref.at[span], load_sem.at[q]))
                 stores[q].start()
+            elif q > 0:
+                moves.append(dispatch(r + 1, q))
             else:
-                moves.append(dispatch(r + 1, q))
+                recv[1][0][g] = cur[pick[1][0], span]
+                finish_early(turned_copies, early)
+                moves.insert(0, [])
     for copy in copies:
         copy.wait_send()
     for copy in stores:
@@ -272,7 +338,7 @@
     slots = factor.shape[1] // W
     chips = members // 2
     stages = chips.bit_length() - 1
-    assert slots == 4 and chips == 1 << stages and stages >= 1
+    assert slots == 4 and chips == 1 << stages and stages >= 1 and ROUNDS == 2
     size = 2 * W
     dma = pltpu.SemaphoreType.DMA
     smem = pl.BlockSpec(memory_space=pltpu.SMEM)
@@ -286,6 +352,10 @@
             pltpu.VMEM((slots, rows, W), F32),
             pltpu.VMEM((ROUNDS, groups - 1, rows, W), F32),
             [[pltpu.VMEM((groups, rows // CHUNKS, W), F32)] * CHUNKS] * ROUNDS,
+            pltpu.VMEM((groups - 1, rows // CHUNKS, size), F32),
+            pltpu.VMEM((groups - 1, rows // CHUNKS, size), F32),
+            pltpu.VMEM((groups - 1, size // members, W), F32),
+            pltpu.VMEM((groups - 1, size, W), F32),
             pltpu.VMEM((2, size, size), F32),
             pltpu.VMEM((ROUNDS, 2 * stages, size + 8, W), F32),
             pltpu.VMEM((ROUNDS, 3, size + 8, W), F32),
@@ -295,6 +365,12 @@
             dma((CHUNKS,)),
             dma((ROUNDS, CHUNKS, groups - 1)),
             dma((ROUNDS, CHUNKS, groups - 1)),
+            dma((groups - 1,)),
+            dma((groups - 1,)),
+            dma((groups - 1,)),
+            dma((groups - 1,)),
+            dma((stages + 1,)),
+            dma((stages + 1,)),
             dma((ROUNDS,)),
             dma((ROUNDS,)),
             dma((ROUNDS, stages, 2)),

time: 132 us -> 129 us (0.977)
  Pallas kernels: 129 us -> 125 us
    pallas_call x1, Pallas kernels: 129 us -> 125 us  [on_device(): pl.pallas_call(functools.partial(kernel, groups, members), out_shape=jax....]
where the time goes in v3:
time: 129 us
  Pallas kernels  125 us (97%)
  local copies, waits for them, and re-layouts  3.08 us (2%)
    pallas_call x1, Pallas kernels, on_device(): pl.pallas_call(functools.partial(kernel, groups, members), out_shape=jax....  125 us
    unnamed x1, local copies, waits for them, and re-layouts  3.08 us

profile of v3, /device:TPU:25, one launch (start us, length us, event | category | flops | bytes accessed | tf_op | source)
XLA Modules:
  0.0 128.6 jit_solution(16658480841042050754)
XLA Ops:
  0.0 125.5 %shard_map.37 = f32[1024,512]{1,0:T(8,128)} custom-call(f32[1024,512]{1,0:T(8,128)} %factor_ref.1, s32[8,16]{1,0:T(8,128)} %bitcast.1, s32[2,16]{1,0:T(2,128)} %plan_ref.1), custom_call_target="tpu_custom_call" | custom-call | tf_op jit(solution)/shard_map/pallas_call | solution.py:345
  125.5 3.1 %copy.5 = f32[1024,512]{1,0:T(8,128)} copy(f32[1024,512]{1,0:T(8,128)} %shard_map.37) | data formatting | bytes 4194304

commit v4 on v3

--- a/solution.py
+++ b/solution.py
@@ -94,7 +94,7 @@
 
 
 def kernel(
-    groups, members, factor_ref, support_ref, plan_ref, out_ref,
+    groups, members, factor_ref, support_ref, plan_ref, out_ref, rot_out,
     held, cur, send, recv, early_out, early_in, turn_out, turns,
     acc, gram, gram_in, rot, rot_pair, stack,
     load_sem, move_send, move_recv, early_send, early_recv, turn_send, turn_recv, spread_send, spread_recv,
@@ -256,12 +256,19 @@
             if r == 0 and q == CHUNKS - 1:
                 early = send_early()
             for k in range(2):
-                high, low = split(load_pair(r, k, q))
+                pair = load_pair(r, k, q)
+                if r == ROUNDS - 1:
+                    held[pl.ds(q * chunk, chunk), k * size:(k + 1) * size] = pair
+                high, low = split(pair)
                 mixed = dot_t(high, low)
                 part = dot_t(high, high) + (mixed + mixed.T)
                 acc[k] = part if q == 0 else acc[k] + part
             if r == 0 and q == 0:
                 stage_early()
+            if r == ROUNDS - 1:
+                span = pl.ds(q * chunk, chunk)
+                stores.append(pltpu.make_async_copy(held.at[span], out_ref.at[span], load_sem.at[q]))
+                stores[q].start()
         for k in range(2):
             cross, tile, diagonal = pack(acc[k])
             gram_in[r, k, :W] = cross
@@ -304,24 +311,21 @@
             device_id_type=MESH,
         ))
         back.wait_recv()
+        if r == ROUNDS - 1:
+            rot_out[core] = rot[r, 0]
+            rot_out[1 - core] = rot[r, 1]
+            break
         rot_pair[core] = rot[r, 0]
         rot_pair[1 - core] = rot[r, 1]
         moves = []
-        if r < ROUNDS - 1:
-            turned_copies = send_turns()
-        for q in (range(CHUNKS) if r == ROUNDS - 1 else [*range(1, CHUNKS), 0]):
+        turned_copies = send_turns()
+        for q in [*range(1, CHUNKS), 0]:
             span = pl.ds(q * chunk, chunk)
             for k in range(2):
                 turned = dot3(load_pair(r, k, q), rot_pair[k])
-                if r == ROUNDS - 1:
-                    held[span, k * size:(k + 1) * size] = turned
-                else:
-                    cur[2 * k, span] = turned[:, :W]
-                    cur[2 * k + 1, span] = turned[:, W:]
-            if r == ROUNDS - 1:
-                stores.append(pltpu.make_async_copy(held.at[span], out_ref.at[span], load_sem.at[q]))
-                stores[q].start()
-            elif q > 0:
+                cur[2 * k, span] = turned[:, :W]
+                cur[2 * k + 1, span] = turned[:, W:]
+            if q > 0:
                 moves.append(dispatch(r + 1, q))
             else:
                 recv[1][0][g] = cur[pick[1][0], span]
@@ -333,6 +337,13 @@
         copy.wait()
 
 
+def rotate_rows(rows_ref, rot_ref, out_ref):
+    size = rot_ref.shape[1]
+    for k in range(2):
+        span = slice(k * size, (k + 1) * size)
+        out_ref[:, span] = dot3(rows_ref[:, span], rot_ref[k])
+
+
 def on_device(groups, members, factor, support, plan):
     rows = factor.shape[0]
     slots = factor.shape[1] // W
@@ -342,11 +353,11 @@
     size = 2 * W
     dma = pltpu.SemaphoreType.DMA
     smem = pl.BlockSpec(memory_space=pltpu.SMEM)
-    return pl.pallas_call(
+    paired, turns = pl.pallas_call(
         functools.partial(kernel, groups, members),
-        out_shape=jax.ShapeDtypeStruct(factor.shape, F32),
+        out_shape=(jax.ShapeDtypeStruct(factor.shape, F32), jax.ShapeDtypeStruct((2, size, size), F32)),
         in_specs=[pl.BlockSpec(memory_space=pl.ANY), smem, smem],
-        out_specs=pl.BlockSpec(memory_space=pl.ANY),
+        out_specs=(pl.BlockSpec(memory_space=pl.ANY), pl.BlockSpec(memory_space=pltpu.VMEM)),
         scratch_shapes=[
             pltpu.VMEM(factor.shape, F32),
             pltpu.VMEM((slots, rows, W), F32),
@@ -382,6 +393,15 @@
             collective_id=0, has_side_effects=True, vmem_limit_bytes=123 * 512 * 1024
         ),
     )(factor, support.T, plan)
+    block = pl.BlockSpec((rows // 4, factor.shape[1]), lambda i: (i, 0))
+    return pl.pallas_call(
+        rotate_rows,
+        grid=(4,),
+        out_shape=jax.ShapeDtypeStruct(factor.shape, F32),
+        in_specs=[block, pl.BlockSpec((2, size, size), lambda i: (0, 0, 0))],
+        out_specs=block,
+        compiler_params=pltpu.CompilerParams(vmem_limit_bytes=123 * 512 * 1024),
+    )(paired, turns)
 
 
 def solution(mesh):

time: 129 us -> 129 us (level)
  Pallas kernels: 125 us -> 129 us
  local copies, waits for them, and re-layouts: 3.08 us -> 0 us
    pallas_call x1 -> x2, Pallas kernels: 125 us -> 129 us  [the longest x1 124 us: on_device(): pl.pallas_call(functools.partial(kernel, groups, members), out_shape=(jax...]
    unnamed x1 -> x0, local copies, waits for them, and re-layouts: 3.08 us -> none
where the time goes in v4:
time: 129 us
  Pallas kernels  129 us (100%)
    pallas_call x1, Pallas kernels, on_device(): pl.pallas_call(functools.partial(kernel, groups, members), out_shape=(jax...  124 us
    pallas_call x1, Pallas kernels, on_device(): pl.pallas_call(rotate_rows, grid=(4,), out_shape=jax.ShapeDtypeStruct(fac...  4.67 us

profile of v4, /device:TPU:25, one launch (start us, length us, event | category | flops | bytes accessed | tf_op | source)
XLA Modules:
  0.0 129.2 jit_solution(8000002538942800231)
XLA Ops:
  0.0 124.5 %shard_map.37 = (f32[1024,512]{1,0:T(8,128)}, f32[2,256,256]{2,1,0:T(8,128)}) custom-call(f32[1024,512]{1,0:T(8,128)} %factor_ref.1, s32[8,16]{1,0:T(8,128)} %bitcast.1, s32[2,16]{1,0:T(2,128)} %plan_ref.1), custom_call_target="tpu_custom_call" | custom-call | tf_op jit(solution)/shard_map/pallas_call | solution.py:356
  124.5 4.7 %shard_map.38 = f32[1024,512]{1,0:T(8,128)} custom-call(f32[1024,512]{1,0:T(8,128)} %get-tuple-element.7.rows_ref, f32[2,256,256]{2,1,0:T(8,128)} %get-tuple-element.8.rot_ref), custom_call_target="tpu_custom_call" | custom-call | tf_op jit(solution)/shard_map/pallas_call | solution.py:397
